TPU v7x, 32 devices: a whole 2x2x4 slice. The times are simulated.
32 devices in a mesh: section: 2 (over y), expert: 16 (over z, x, core).
Axes of the slice: x: 2, y: 2, z: 4, core: 2. Of those that a mesh axis runs over, the one named last changes fastest.
Arguments:
- inputs: bfloat16 [2, 64, 4096], P(None, None, 'expert'), may hold values from -6 to 6
- expert_ids: int32 [64, 2, 2], P('expert'), may hold values from 0 to 7, all different within a row; in each aligned block of 8 rows (0 to 7, 8 to 15, ..., all dimensions but the last counted through in order) at most 2 rows name the same one
- mamba_gain: float32 [2, 4096], P('section', 'expert'), may hold values from 0.1 to 1.9
- dt_in: bfloat16 [2, 4096, 256], P('section', 'expert'), may hold values from -0.09375 to 0.09375
- dt_out: bfloat16 [2, 256, 4096], P('section', None, 'expert'), may hold values from -0.375 to 0.375
- dt_bias: float32 [2, 4096], P('section', 'expert'), may hold values from -5 to 0
- state_in: bfloat16 [2, 4096, 32], P('section', 'expert'), may hold values from -0.09375 to 0.09375
- decay_rate: float32 [2, 4096, 16], P('section', 'expert'), may hold values from 0.02 to 2
- skip_gain: float32 [2, 4096], P('section', 'expert'), may hold values from 0.5 to 1.5
- moe_gain: float32 [4096], replicated, may hold values from 0.1 to 1.9
- router: bfloat16 [4096, 8], replicated, may hold values from -0.25 to 0.25
- expert_in: bfloat16 [2, 4096, 98304], P(None, 'section', 'expert'), may hold values from -0.09375 to 0.09375
- expert_out: bfloat16 [98304, 4096], P('expert', 'section'), may hold values from -0.21875 to 0.21875
Outputs:
- layer_out: bfloat16 [2, 64, 4096], P(None, 'expert', 'section')
Inputs may be any that keep to these rules, and one draw needn't show every extreme that they name: `expert_ids`: within each aligned block of 8 rows of the first two dimensions taken together, every expert is named exactly 2 times; a row names 2 different experts.
All inputs are finite; a program needn't handle non-finite values.
Results may differ from a plain program's by a relative error of at most 0.029.
Values may be sent and summed in bfloat16 or wider, within the bound.
A program may use at most 192 MiB of HBM per device.

v0:
```python
import jax
import jax.numpy as jnp
from jax import lax
from jax.sharding import PartitionSpec as P


def passed_along(array, axis, by):
    peers = lax.axis_size(axis)
    pairs = [(i, i + by) for i in range(peers) if 0 <= i + by < peers]
    return lax.ppermute(array, axis, pairs)


def from_root(array, axis, root):
    mine = lax.axis_index(axis) == root
    return lax.psum(jnp.where(mine, array, jnp.zeros_like(array)), axis)


def normed(values, gain):
    return values * lax.rsqrt(jnp.mean(values * values, axis=-1, keepdims=True) + 1e-05) * gain


def scan_rows(step_dt, u_float, b_in, c_out, rate_w):
    row_count = step_dt.shape[0]
    blocks = row_count // 16
    pieces = (
        step_dt.reshape(blocks, 16, -1),
        u_float.reshape(blocks, 16, -1),
        b_in.reshape(blocks, 16, -1),
        c_out.reshape(blocks, 16, -1),
    )

    def advance(carried, block_pieces):
        dt_block, u_block, b_block, c_block = block_pieces
        emitted = []
        for index in range(16):
            carried = (
                jnp.exp(-dt_block[index][:, None] * rate_w) * carried
                + (dt_block[index] * u_block[index])[:, None] * b_block[index][None, :]
            )
            emitted.append(jnp.sum(carried * c_block[index][None, :], axis=1))
        return (carried, jnp.stack(emitted))

    begin = jnp.zeros(rate_w.shape, jnp.float32)
    _, mixed = lax.scan(advance, begin, pieces)
    return mixed.reshape(row_count, -1)


def mamba_layer(hidden_in, gain, dt_in_w, dt_out_w, bias_w, state_w, rate_w, skip_w):
    state_size = rate_w.shape[1]
    full_width = hidden_in.shape[1] * lax.axis_size("expert")
    hidden_f = hidden_in.astype(jnp.float32)
    squares = lax.psum(jnp.sum(hidden_f * hidden_f, axis=1), "expert")
    scale = lax.rsqrt(squares / full_width + 1e-05)
    normed_u = (hidden_f * scale[:, None] * gain).astype(jnp.bfloat16)
    low_part = jnp.dot(normed_u, dt_in_w, preferred_element_type=jnp.float32)
    state_part = jnp.dot(normed_u, state_w, preferred_element_type=jnp.float32)
    low_sum, state_sum = lax.psum((low_part, state_part), "expert")
    low_rank = low_sum.astype(jnp.bfloat16)
    step_dt = jax.nn.softplus(
        jnp.dot(low_rank, dt_out_w, preferred_element_type=jnp.float32) + bias_w
    )
    b_in = state_sum[:, :state_size]
    c_out = state_sum[:, state_size:]
    u_float = normed_u.astype(jnp.float32)
    mixed = scan_rows(step_dt, u_float, b_in, c_out, rate_w)
    output = mixed + skip_w * u_float
    return (hidden_f + output * jax.nn.silu(u_float)).astype(jnp.bfloat16)


def moe_layer(hidden, ids, gain, router_w, in_w, out_w):
    batches, tok_rows, full_width = hidden.shape
    experts = router_w.shape[1]
    top_count = ids.shape[2]
    devices = lax.axis_size("expert")
    group = devices // experts
    slice_width = in_w.shape[1]
    section_here = lax.axis_index("section")
    capacity = tok_rows * batches * top_count // experts
    ordered = hidden.transpose(1, 0, 2).reshape(-1, full_width)
    hidden_f = ordered.astype(jnp.float32)
    normed_u = normed(hidden_f, gain).astype(jnp.bfloat16)
    probs = jax.nn.softmax(jnp.dot(normed_u, router_w, preferred_element_type=jnp.float32), axis=-1)
    id_rows = ids.reshape(-1, top_count)
    picked = jnp.take_along_axis(probs, id_rows, axis=1)
    weights = picked / jnp.sum(picked, axis=1, keepdims=True)
    flat_ids = ids.reshape(-1)
    onehot = (flat_ids[:, None] == jnp.arange(experts, dtype=jnp.int32)[None, :]).astype(jnp.int32)
    ranks = jnp.sum((jnp.cumsum(onehot, axis=0) - onehot) * onehot, axis=1)
    slots = flat_ids * capacity + ranks
    place = (slots[None, :] == jnp.arange(experts * capacity, dtype=jnp.int32)[:, None]).astype(
        jnp.bfloat16
    )
    repeated = jnp.repeat(normed_u, top_count, axis=0)
    packed = jnp.dot(place, repeated, preferred_element_type=jnp.float32).astype(jnp.bfloat16)
    my_features = lax.dynamic_slice_in_dim(packed, section_here * slice_width, slice_width, 1)
    outgoing = jnp.broadcast_to(
        my_features.reshape(experts, 1, capacity, slice_width),
        (experts, group, capacity, slice_width),
    ).reshape(devices, capacity, slice_width)
    arrived = lax.all_to_all(outgoing, "expert", split_axis=0, concat_axis=0, tiled=True)
    rows_in = arrived.reshape(-1, slice_width)
    gate_part = jnp.dot(rows_in, in_w[0], preferred_element_type=jnp.float32)
    up_part = jnp.dot(rows_in, in_w[1], preferred_element_type=jnp.float32)
    gate_sum, up_sum = (
        lax.psum(gate_part.astype(jnp.bfloat16), "section").astype(jnp.float32),
        lax.psum(up_part.astype(jnp.bfloat16), "section").astype(jnp.float32),
    )
    units = (jax.nn.silu(gate_sum) * up_sum).astype(jnp.bfloat16)
    produced = jnp.dot(units, out_w, preferred_element_type=jnp.float32).astype(jnp.bfloat16)
    finished = lax.all_to_all(
        produced.reshape(devices, capacity, slice_width),
        "expert",
        split_axis=0,
        concat_axis=0,
        tiled=True,
    )
    summed = jnp.sum(
        finished.reshape(experts, group, capacity, slice_width).astype(jnp.float32), axis=1
    )
    lookup = summed.reshape(experts * capacity, slice_width)
    chosen = lookup[slots].reshape(-1, top_count, slice_width)
    routed = jnp.sum(chosen * weights[:, :, None], axis=1)
    residual = lax.dynamic_slice_in_dim(hidden_f, section_here * slice_width, slice_width, 1)
    mixed_out = (residual + routed).astype(jnp.bfloat16)
    return mixed_out.reshape(tok_rows, batches, slice_width).transpose(1, 0, 2)


def shards(
    inputs,
    expert_ids,
    mamba_gain,
    dt_in,
    dt_out,
    dt_bias,
    state_in,
    decay_rate,
    skip_gain,
    moe_gain,
    router,
    expert_in,
    expert_out,
):
    sections = lax.axis_size("section")
    section_here = lax.axis_index("section")
    batches = inputs.shape[0]

    def tick(moment, carried):
        received, results = carried
        batch_index = moment - section_here
        active = jnp.logical_and(batch_index >= 0, batch_index < batches)
        clipped = jnp.clip(batch_index, 0, batches - 1)
        first_rows = lax.dynamic_index_in_dim(inputs, clipped, 0, keepdims=False)
        current = jnp.where(section_here == 0, first_rows, received)
        produced = mamba_layer(
            current,
            mamba_gain[0],
            dt_in[0],
            dt_out[0],
            dt_bias[0],
            state_in[0],
            decay_rate[0],
            skip_gain[0],
        )
        updated = lax.dynamic_update_index_in_dim(results, produced, clipped, 0)
        results = jnp.where(active, updated, results)
        passed = passed_along(produced, "section", 1)
        return (passed, results)

    begin = (jnp.zeros(inputs.shape[1:], jnp.bfloat16), jnp.zeros(inputs.shape, jnp.bfloat16))
    _, results = lax.fori_loop(0, batches + sections - 1, tick, begin)
    finals = from_root(results, "section", sections - 1)
    hidden = lax.all_to_all(finals, "expert", split_axis=1, concat_axis=2, tiled=True)
    return moe_layer(hidden, expert_ids, moe_gain, router, expert_in, expert_out)


def solution(mesh):
    placed = (
        P(None, None, "expert"),
        P("expert", None, None),
        P("section", "expert"),
        P("section", "expert", None),
        P("section", None, "expert"),
        P("section", "expert"),
        P("section", "expert", None),
        P("section", "expert", None),
        P("section", "expert"),
        P(),
        P(),
        P(None, "section", "expert"),
        P("expert", "section"),
    )
    return jax.shard_map(
        shards, mesh=mesh, in_specs=placed, out_specs=P(None, "expert", "section"), check_vma=False
    )
```

profile of v0, /device:TPU:0, one launch (start us, length us, event | category | flops | bytes accessed | tf_op | source)
XLA Modules:
  0.0 501.1 jit_solution(2239321044366703222)
XLA Ops:
  6.6 359.1 %while.45 = (s32[]{:T(128)}, bf16[64,256]{1,0:T(8,128)(2,1)S(1)}, bf16[2,64,256]{2,1,0:T(8,128)(2,1)S(1)}, pred[]{:T(512)}, s32[]{:T(128)}, /*index=5*/bf16[2,64...) while((s32[]{:T(128)}, bf16[64,256]{1,0:T(8,128)(2,1)S(1)}, ...), condition=%wide.region_23.24_spmd, body=%wide.region_0.23_spmd.sunk | while | flops 19069084 | bytes 1702200 | solution.py:170
  7.5 34.9 %psum.61 = f32[64]{0:T(128)S(1)} all-reduce(f32[64]{0:T(128)S(1)} %get-tuple-element.835), channel_id=1, replica_groups=mesh['section'=2,'expert'=16] {'expert'}, use_global_device_ids=true, to_apply=%region_2.2 | all-reduce | flops 64 | bytes 512 | tf_op jit(solution)/shard_map/while/body/eval_jaxpr/psum | solution.py:52
  45.2 58.4 %all-reduce.3 = (bf16[64,256]{1,0:T(8,128)(2,1)S(1)}, f32[64,32]{0,1:T(8,128)S(1)}) all-reduce(f32[64,256]{1,0:T(8,128)S(1)} %fusion.144, f32[64,32]{0,1:T(8,128)S(1)} %fusion.145), channel_id=1, replica_groups=mesh['section'=2,'expert'=16] {'expert'}, use_global_device_ids=true, to_apply=%region_3.3 | all-reduce | flops 18432 | bytes 114688 | tf_op jit(solution)/shard_map/while/body/eval_jaxpr/psum | solution.py:57
  104.9 18.6 %while.46 = (s32[]{:T(128)}, f32[256,16]{0,1:T(8,128)S(1)}, f32[4,16,256]{2,1,0:T(8,128)S(1)}, f32[4,16,256]{2,1,0:T(8,128)S(1)}, f32[256,16]{0,1:T(8,128)}, /*i...) while((s32[]{:T(128)}, f32[256,16]{0,1:T(8,128)S(1)}, ...), condition=%wide.region_22.22_spmd.clone, body=%wide.region_5.21_spmd.clone.sunk | while | flops 585746 | bytes 505056 | solution.py:44
  124.4 3.4 collective-permute-start
  130.3 29.5 %psum.61 = f32[64]{0:T(128)S(1)} all-reduce(f32[64]{0:T(128)S(1)} %get-tuple-element.835), channel_id=1, replica_groups=mesh['section'=2,'expert'=16] {'expert'}, use_global_device_ids=true, to_apply=%region_2.2 | all-reduce | flops 64 | bytes 512 | tf_op jit(solution)/shard_map/while/body/eval_jaxpr/psum | solution.py:52
  162.6 58.4 %all-reduce.3 = (bf16[64,256]{1,0:T(8,128)(2,1)S(1)}, f32[64,32]{0,1:T(8,128)S(1)}) all-reduce(f32[64,256]{1,0:T(8,128)S(1)} %fusion.144, f32[64,32]{0,1:T(8,128)S(1)} %fusion.145), channel_id=1, replica_groups=mesh['section'=2,'expert'=16] {'expert'}, use_global_device_ids=true, to_apply=%region_3.3 | all-reduce | flops 18432 | bytes 114688 | tf_op jit(solution)/shard_map/while/body/eval_jaxpr/psum | solution.py:57
  222.2 18.6 %while.46 = (s32[]{:T(128)}, f32[256,16]{0,1:T(8,128)S(1)}, f32[4,16,256]{2,1,0:T(8,128)S(1)}, f32[4,16,256]{2,1,0:T(8,128)S(1)}, f32[256,16]{0,1:T(8,128)}, /*i...) while((s32[]{:T(128)}, f32[256,16]{0,1:T(8,128)S(1)}, ...), condition=%wide.region_22.22_spmd.clone, body=%wide.region_5.21_spmd.clone.sunk | while | flops 585746 | bytes 505056 | solution.py:44
  241.7 4.2 collective-permute-start
  248.4 29.5 %psum.61 = f32[64]{0:T(128)S(1)} all-reduce(f32[64]{0:T(128)S(1)} %get-tuple-element.835), channel_id=1, replica_groups=mesh['section'=2,'expert'=16] {'expert'}, use_global_device_ids=true, to_apply=%region_2.2 | all-reduce | flops 64 | bytes 512 | tf_op jit(solution)/shard_map/while/body/eval_jaxpr/psum | solution.py:52
  280.7 58.4 %all-reduce.3 = (bf16[64,256]{1,0:T(8,128)(2,1)S(1)}, f32[64,32]{0,1:T(8,128)S(1)}) all-reduce(f32[64,256]{1,0:T(8,128)S(1)} %fusion.144, f32[64,32]{0,1:T(8,128)S(1)} %fusion.145), channel_id=1, replica_groups=mesh['section'=2,'expert'=16] {'expert'}, use_global_device_ids=true, to_apply=%region_3.3 | all-reduce | flops 18432 | bytes 114688 | tf_op jit(solution)/shard_map/while/body/eval_jaxpr/psum | solution.py:57
  340.4 18.6 %while.46 = (s32[]{:T(128)}, f32[256,16]{0,1:T(8,128)S(1)}, f32[4,16,256]{2,1,0:T(8,128)S(1)}, f32[4,16,256]{2,1,0:T(8,128)S(1)}, f32[256,16]{0,1:T(8,128)}, /*i...) while((s32[]{:T(128)}, f32[256,16]{0,1:T(8,128)S(1)}, ...), condition=%wide.region_22.22_spmd.clone, body=%wide.region_5.21_spmd.clone.sunk | while | flops 585746 | bytes 505056 | solution.py:44
  359.9 4.2 collective-permute-start
  366.9 18.5 %all-reduce.7.cloned.1.call-done = bf16[2,64,256]{2,0,1:T(2,128)(2,1)} async-done(((bf16[2,64,256]{2,0,1:T(2,128)(2,1)}), bf16[2,64,256]{2,0,1:T(2,128)(2,1)}) %all-reduce.7.cloned.1.call-update) | async-done | bytes 65552 | tf_op jit(solution)/shard_map/psum | solution.py:15
  385.4 5.6 %all-to-all-start = ((bf16[2,64,256]{2,0,1:T(2,128)(2,1)}), bf16[2,64,256]{2,0,1:T(2,128)(2,1)S(1)}, u32[]{:S(2)}, u32[]{:S(2)}) async-start(bf16[2,64,256]{2,0,1:T(2,128)(2,1)} %all-reduce.7.cloned.1.call-done), calls=%async_computation | async-start | bytes 131072 | tf_op jit(solution)/shard_map/all_to_all | solution.py:172
  391.0 6.9 %all-to-all-done = bf16[2,64,256]{2,0,1:T(2,128)(2,1)S(1)} async-done(((bf16[2,64,256]{2,0,1:T(2,128)(2,1)}), bf16[2,64,256]{2,0,1:T(2,128)(2,1)S(1)}, u32[]{:S(2)}, u32[]{:S(2)}) %all-to-all-start) | async-done | bytes 65568 | tf_op jit(solution)/shard_map/all_to_all | solution.py:172
  399.9 3.5 all-to-all-start.1
  403.8 7.5 %all-to-all-done.1 = bf16[16,2,2048]{2,1,0:T(2,128)(2,1)S(1)} async-done(((bf16[16,2,2048]{2,1,0:T(2,128)(2,1)}), bf16[16,2,2048]{2,1,0:T(2,128)(2,1)S(1)}, u32[]{:S(2)}, u32[]{:S(2)}) %all-to-all-start.1) | async-done | bytes 131104 | tf_op jit(solution)/shard_map/all_to_all | solution.py:100
  411.3 11.2 %fusion.88 = bf16[32,6144]{1,0:T(8,128)(2,1)} fusion(bf16[32,2048]{1,0:T(8,128)(2,1)S(1)} %reshape.645, bf16[2,2048,6144]{2,1,0:T(8,128)(2,1)} %param.28), kind=kOutput, calls=%fused_computation.192 | convolution fusion | flops 805502976 | bytes 25690112 | tf_op jit(solution)/shard_map/dot_general | solution.py:102
  422.6 11.2 %fusion.91 = bf16[32,6144]{1,0:T(8,128)(2,1)} fusion(bf16[32,2048]{1,0:T(8,128)(2,1)S(1)} %reshape.645, bf16[2,2048,6144]{2,1,0:T(8,128)(2,1)} %param.28), kind=kOutput, calls=%fused_computation.193 | convolution fusion | flops 805502976 | bytes 25690112 | tf_op jit(solution)/shard_map/dot_general | solution.py:103
  435.1 30.1 %all-reduce.9.cloned.1.call-done = (bf16[32,6144]{1,0:T(8,128)(2,1)}, bf16[32,6144]{1,0:T(8,128)(2,1)}) async-done(((bf16[32,6144]{1,0:T(8,128)(2,1)}, bf16[32,6144]{1,0:T(8,128)(2,1)}), (bf16[32,6144]{1,0:T(8,128)(2,1)}, bf16[32,6144]{1,0:T(8,128)(2,1)})) %all-reduce.9.cloned.1.call-update) | async-done | bytes 786448 | tf_op jit(solution)/shard_map/psum | solution.py:106
  465.2 12.8 %convolution_convert_fusion = bf16[32,2048]{1,0:T(8,128)(2,1)S(1)} fusion(bf16[6144,2048]{1,0:T(8,128)(2,1)} %param.29, bf16[32,6144]{1,0:T(8,128)(2,1)} %get-tuple-element.507, bf16[32,6144]{1,0:T(8,128)(2,1)} %get-tuple-element.508), kind=kOutput, calls=%fused_computation.194 | convolution fusion | flops 806944768 | bytes 26083328 | tf_op jit(solution)/shard_map/dot_general | solution.py:109
  478.8 5.6 %all-to-all-start.2 = ((bf16[16,2,2048]{2,1,0:T(2,128)(2,1)}), bf16[16,2,2048]{2,1,0:T(2,128)(2,1)S(1)}, u32[]{:S(2)}, u32[]{:S(2)}) async-start(bf16[16,2,2048]{2,1,0:T(2,128)(2,1)} %reshape.646), calls=%async_computation.2 | async-start | bytes 262144 | tf_op jit(solution)/shard_map/all_to_all | solution.py:110
  484.9 7.5 %all-to-all-done.2 = bf16[16,2,2048]{2,1,0:T(2,128)(2,1)S(1)} async-done(((bf16[16,2,2048]{2,1,0:T(2,128)(2,1)}), bf16[16,2,2048]{2,1,0:T(2,128)(2,1)S(1)}, u32[]{:S(2)}, u32[]{:S(2)}) %all-to-all-start.2) | async-done | bytes 131104 | tf_op jit(solution)/shard_map/all_to_all | solution.py:110
  (228 shorter events, 85.2 us)
Async XLA Ops:
  6.5 427.5 %copy-start = (bf16[4096,8]{0,1:T(8,128)(2,1)S(1)}, bf16[4096,8]{0,1:T(8,128)(2,1)}, u32[]{:S(2)}) copy-start(bf16[4096,8]{0,1:T(8,128)(2,1)} %param.27) | copy-start | bytes 196612
  6.5 359.9 %copy-start.1 = (s32[4,2,2]{0,2,1:T(2,128)S(1)}, s32[4,2,2]{0,2,1:T(2,128)}, u32[]{:S(2)}) copy-start(s32[4,2,2]{0,2,1:T(2,128)} %param.18) | copy-start | bytes 196
  6.5 392.1 %copy-start.2 = (f32[4096]{0:T(1024)S(1)}, f32[4096]{0:T(1024)}, u32[]{:S(2)}) copy-start(f32[4096]{0:T(1024)} %param.26) | copy-start | bytes 49156
  6.5 378.9 %all-reduce.7.cloned.1.call-start = ((), (), s32[]{:S(2)}) async-start(), calls=%async_computation.3 | async-start | bytes 131072 | tf_op jit(solution)/shard_map/psum | solution.py:15
  124.4 5.0 %collective-permute-start = (bf16[64,256]{1,0:T(8,128)(2,1)S(1)}, bf16[64,256]{1,0:T(8,128)(2,1)S(1)}, u32[]{:S(2)}, u32[]{:S(2)}) collective-permute-start(bf16[64,256]{1,0:T(8,128)(2,1)S(1)} %get-tuple-element.842), channel_id=1, source_target_pairs={{0,16},{1,17},{2,18},{3,19},{4,20},{5,21},{6,22},{7,23},{8,24},{9,... | collective-permute-start | bytes 98312 | tf_op jit(solution)/shard_map/while/body/eval_jaxpr/ppermute | solution.py:10
  241.7 5.8 %collective-permute-start = (bf16[64,256]{1,0:T(8,128)(2,1)S(1)}, bf16[64,256]{1,0:T(8,128)(2,1)S(1)}, u32[]{:S(2)}, u32[]{:S(2)}) collective-permute-start(bf16[64,256]{1,0:T(8,128)(2,1)S(1)} %get-tuple-element.842), channel_id=1, source_target_pairs={{0,16},{1,17},{2,18},{3,19},{4,20},{5,21},{6,22},{7,23},{8,24},{9,... | collective-permute-start | bytes 98312 | tf_op jit(solution)/shard_map/while/body/eval_jaxpr/ppermute | solution.py:10
  359.9 5.8 %collective-permute-start = (bf16[64,256]{1,0:T(8,128)(2,1)S(1)}, bf16[64,256]{1,0:T(8,128)(2,1)S(1)}, u32[]{:S(2)}, u32[]{:S(2)}) collective-permute-start(bf16[64,256]{1,0:T(8,128)(2,1)S(1)} %get-tuple-element.842), channel_id=1, source_target_pairs={{0,16},{1,17},{2,18},{3,19},{4,20},{5,21},{6,22},{7,23},{8,24},{9,... | collective-permute-start | bytes 98312 | tf_op jit(solution)/shard_map/while/body/eval_jaxpr/ppermute | solution.py:10
  385.4 12.5 %all-to-all-start = ((bf16[2,64,256]{2,0,1:T(2,128)(2,1)}), bf16[2,64,256]{2,0,1:T(2,128)(2,1)S(1)}, u32[]{:S(2)}, u32[]{:S(2)}) async-start(bf16[2,64,256]{2,0,1:T(2,128)(2,1)} %all-reduce.7.cloned.1.call-done), calls=%async_computation | async-start | bytes 131072 | tf_op jit(solution)/shard_map/all_to_all | solution.py:172
  399.9 11.4 %all-to-all-start.1 = ((bf16[16,2,2048]{2,1,0:T(2,128)(2,1)}), bf16[16,2,2048]{2,1,0:T(2,128)(2,1)S(1)}, u32[]{:S(2)}, u32[]{:S(2)}) async-start(bf16[16,2,2048]{2,1,0:T(2,128)(2,1)} %bitcast.19), calls=%async_computation.1 | async-start | bytes 262144 | tf_op jit(solution)/shard_map/all_to_all | solution.py:100
  403.4 61.8 %all-reduce.9.cloned.1.call-start = ((), (), s32[]{:S(2)}) async-start(), calls=%async_computation.4 | async-start | bytes 1572864 | tf_op jit(solution)/shard_map/psum | solution.py:106
  478.8 13.6 %all-to-all-start.2 = ((bf16[16,2,2048]{2,1,0:T(2,128)(2,1)}), bf16[16,2,2048]{2,1,0:T(2,128)(2,1)S(1)}, u32[]{:S(2)}, u32[]{:S(2)}) async-start(bf16[16,2,2048]{2,1,0:T(2,128)(2,1)} %reshape.646), calls=%async_computation.2 | async-start | bytes 262144 | tf_op jit(solution)/shard_map/all_to_all | solution.py:110
Sparse Core Ops, SparseCore 0:
  366.5 18.8 all-reduce.6
  433.9 31.2 all-reduce.8
where the time goes:
time: 508 us; the launch traced here: 501 us
  blocking collectives  269 us (53%)
  waiting for transfers between devices  75.2 us (15%)
  other arithmetic  61.6 us (12%)
  matrix products  45 us (9%)
  starting transfers between devices  26.7 us (5%)
  between operations  13.6 us (3%)
  local copies, waits for them, and re-layouts  9.09 us (2%)
    psum x3, blocking collectives, mamba_layer(): low_sum, state_sum = lax.psum((low_part, state_part), 'expert')  175 us
    psum x3, blocking collectives, mamba_layer(): squares = lax.psum(jnp.sum(hidden_f * hidden_f, axis=1), 'expert')  93.9 us
    reduce_sum x60, other arithmetic, advance(): emitted.append(jnp.sum(carried * c_block[index][None, :], axis=1))  50.5 us
    psum x1, waiting for transfers between devices, moe_layer(): lax.psum(up_part.astype(jnp.bfloat16), 'section').astype(jnp.float32)  30.1 us
    psum x1, waiting for transfers between devices, from_root(): return lax.psum(jnp.where(mine, array, jnp.zeros_like(array)), axis)  18.5 us
    dot_general x1, matrix products, moe_layer(): jnp.dot(units, out_w, preferred_element_type=jnp.float32)  12.8 us
    ppermute x3, starting transfers between devices, passed_along(): return lax.ppermute(array, axis, pairs)  11.9 us
    dot_general x1, matrix products, moe_layer(): gate_part = jnp.dot(rows_in, in_w[0], preferred_element_type=jnp.float32)  11.2 us
  transfers between devices with their start and end apart: 8, of which 8 were waited for; matrix products, arithmetic and copies ran while one was open for 1% of the time, Pallas kernels for 0%

commit v1 on v0

--- a/solution.py
+++ b/solution.py
@@ -1,6 +1,10 @@
+import functools
+
 import jax
 import jax.numpy as jnp
 from jax import lax
+from jax.experimental import pallas as pl
+from jax.experimental.pallas import tpu as pltpu
 from jax.sharding import PartitionSpec as P
 
 
@@ -173,6 +177,564 @@
     return moe_layer(hidden, expert_ids, moe_gain, router, expert_in, expert_out)
 
 
+MESH = pl.DeviceIdType.MESH
+STEP_COLUMNS = 512
+IN_SLOTS = 9
+OUT_SLOTS = 7
+WIDE = 384
+
+
+def iota(shape, dim):
+    return lax.broadcasted_iota(jnp.int32, shape, dim)
+
+
+def kernel(
+    inputs, ids, gain, dt_in, dt_out, bias, state_w, rate, skip, moe_gain, router, w_in, w_out,
+    out,
+    win, wout, part, rs_buf, summed, ag_buf, third, step_ref, du_ref, mixed_ref, b_ref, c_ref,
+    own, relay, slot_buf, stat_buf, xsend, xrow, rsend, resid, parts, theirs, units, acc, ret, back,
+    in_sem, out_sem, rs_send, rs_recv, ag_send, ag_recv, relay_send, relay_recv,
+    slot_send, slot_recv, stat_send, stat_recv, x_send, x_recv, r_send, r_recv,
+    p_send, p_recv, u_send, u_recv, b_send, b_recv,
+):
+    f32, bf16 = jnp.float32, jnp.bfloat16
+    peers = lax.axis_size("expert")
+    sec, me = lax.axis_index("section"), lax.axis_index("expert")
+    partner = (1 - sec, me)
+    batches, seq, chans = inputs.shape
+    rows = batches * seq
+    chips = peers // 2
+    full = chans * peers
+    steps = w_in.shape[2] // STEP_COLUMNS
+    half = steps // 2
+
+    def remote(src, dst, ssem, rsem, device):
+        return pltpu.make_async_remote_copy(
+            src_ref=src, dst_ref=dst, send_sem=ssem, recv_sem=rsem,
+            device_id=device, device_id_type=MESH,
+        )
+
+    def in_copy(n):
+        chunk = lax.rem(n + (1 - sec) * half, steps)
+        slot = lax.rem(n, IN_SLOTS)
+        at = pl.multiple_of(chunk * STEP_COLUMNS, STEP_COLUMNS)
+        return pltpu.make_async_copy(
+            w_in.at[:, :, pl.ds(at, STEP_COLUMNS)], win.at[slot], in_sem.at[slot]
+        )
+
+    def out_copy(n):
+        chunk = lax.rem(n + sec * half, steps)
+        slot = lax.rem(n, OUT_SLOTS)
+        at = pl.multiple_of(chunk * STEP_COLUMNS, STEP_COLUMNS)
+        return pltpu.make_async_copy(
+            w_out.at[pl.ds(at, STEP_COLUMNS), :], wout.at[slot], out_sem.at[slot]
+        )
+
+    def loop(first, last, body):
+        def step(n, none):
+            body(n)
+            return none
+        lax.fori_loop(first, last, step, 0)
+
+    barrier = pltpu.get_barrier_semaphore()
+    total = 2 * peers
+
+    def greet(n):
+        line = lax.rem(sec * peers + me + n, total)
+        pl.semaphore_signal(
+            barrier, inc=1, device_id=(line // peers, lax.rem(line, peers)), device_id_type=MESH
+        )
+
+    loop(1, total, greet)
+    loop(0, IN_SLOTS, lambda n: in_copy(n).start())
+    loop(0, OUT_SLOTS, lambda n: out_copy(n).start())
+
+    lane, sub = iota((16, 128), 1), iota((16, 128), 0)
+    across, down = jnp.full((16, 128), -1, jnp.int32), jnp.full((16, 128), -2, jnp.int32)
+    for j in range(16):
+        value = ids[j // 4, (j // 2) % 2, j % 2]
+        across = jnp.where(lane == j, value, across)
+        down = jnp.where(sub == j, value, down)
+    earlier = jnp.where((across == down) & (sub < lane), 1.0, 0.0)
+    rank = jnp.sum(earlier, axis=0, keepdims=True)
+    slot_row = across[:1].astype(f32) * 2.0 + rank
+    slot_buf[me] = jnp.broadcast_to(slot_row, (8, 128))
+    pl.semaphore_wait(barrier, total - 1)
+
+    def slot_copy(n):
+        return remote(
+            slot_buf.at[me], slot_buf.at[me], slot_send.at[n], slot_recv.at[me],
+            (sec, lax.rem(me + n, peers)),
+        )
+
+    loop(1, peers, lambda n: slot_copy(n).start())
+
+    @pl.when(sec == 1)
+    def _():
+        remote(own, relay, relay_send, relay_recv, partner).wait_recv()
+
+    first = inputs[...].reshape(rows, chans)
+    h = jnp.where(sec == 0, first.astype(f32), relay[...].astype(f32))
+    scaled = h * gain[...]
+    scaled_b = scaled.astype(bf16)
+    squares = jnp.sum(h * h, axis=1, keepdims=True)
+    high = squares.astype(bf16).astype(f32)
+    lanes = iota((rows, 128), 1)
+    third[...] = jnp.where(lanes == 32, high, jnp.where(lanes == 33, squares - high, 0.0))
+    third[:, :32] = jnp.dot(scaled_b, state_w[0], preferred_element_type=f32)
+    low = jnp.dot(scaled_b, dt_in[0], preferred_element_type=f32)
+    part[:, :256] = low.astype(bf16)
+    part[:, 256:] = third[...].astype(bf16)
+
+    def rs_copy(n):
+        chip = lax.rem(me // 2 + n, chips)
+        at = pl.multiple_of(chip * 16, 16)
+        return remote(
+            part.at[pl.ds(at, 16)], rs_buf.at[me], rs_send.at[n], rs_recv.at[me], (sec, chip * 2)
+        )
+
+    odd = lax.rem(me, 2) == 1
+
+    @pl.when(odd)
+    def _():
+        rs_copy(0).start()
+
+    loop(1, chips, lambda n: rs_copy(n).start())
+
+    def ag_copy(n):
+        at = pl.multiple_of(me // 2 * 16, 16)
+        return remote(
+            summed, ag_buf.at[pl.ds(at, 16)], ag_send.at[n], ag_recv.at[me // 2],
+            (sec, lax.rem(me + n, peers)),
+        )
+
+    def rs_arrived(source):
+        return remote(part.at[pl.ds(0, 16)], rs_buf.at[source], rs_send.at[0], rs_recv.at[source], (sec, me))
+
+    @pl.when(jnp.logical_not(odd))
+    def _():
+        at = pl.multiple_of(me // 2 * 16, 16)
+        rs_buf[me] = part[pl.ds(at, 16), :]
+        loop(1, peers, lambda n: rs_arrived(lax.rem(me + n, peers)).wait_recv())
+        whole = jnp.sum(rs_buf[...].astype(f32), axis=0)
+        square = whole[:, 288:289] + whole[:, 289:290]
+        scale = lax.rsqrt(square / full + 1e-05)
+        scale_high = scale.astype(bf16).astype(f32)
+        lane3 = iota((16, WIDE), 1)
+        result = jnp.where(
+            lane3 == 288, scale_high, jnp.where(lane3 == 289, scale - scale_high, whole * scale)
+        )
+        summed[...] = result.astype(bf16)
+        ag_buf[pl.ds(at, 16), :] = summed[...]
+        loop(1, peers, lambda n: ag_copy(n).start())
+
+    def ag_arrived(chip):
+        at = pl.multiple_of(chip * 16, 16)
+        return remote(summed, ag_buf.at[pl.ds(at, 16)], ag_send.at[0], ag_recv.at[chip], (sec, me))
+
+    @pl.when(odd)
+    def _():
+        ag_arrived(me // 2).wait_recv()
+
+    loop(1, chips, lambda n: ag_arrived(lax.rem(me // 2 + n, chips)).wait_recv())
+
+    tail = ag_buf[:, 256:]
+    tail_f = tail.astype(f32)
+    scale = tail_f[:, 32:33] + tail_f[:, 33:34]
+    u = (scaled_of(h, scale, gain[...])).astype(bf16).astype(f32)
+    step_pre = jnp.dot(ag_buf[:, :256], dt_out[0], preferred_element_type=f32) + bias[...]
+    step_dt = jnp.maximum(step_pre, 0.0) + jnp.log1p(jnp.exp(-jnp.abs(step_pre)))
+    step_ref[...] = step_dt
+    du_ref[...] = step_dt * u
+    spread = jnp.where(iota((rows * 16, rows), 0) >> 4 == iota((rows * 16, rows), 1), 1.0, 0.0)
+    repeated = jnp.dot(spread.astype(bf16), tail, preferred_element_type=f32)
+    state_lane = iota((rows * 16, 128), 1)
+    state_row = iota((rows * 16, 128), 0) & 15
+    ones = jnp.ones((128, 128), bf16)
+    b_ref[...] = jnp.dot(
+        jnp.where(state_lane == state_row, repeated, 0.0).astype(bf16), ones,
+        preferred_element_type=f32,
+    )
+    c_ref[...] = jnp.dot(
+        jnp.where(state_lane == state_row + 16, repeated, 0.0).astype(bf16), ones,
+        preferred_element_type=f32,
+    )
+    negative = -jnp.transpose(rate[0])
+
+    def advance(t, states):
+        after = []
+        for m in range(batches):
+            row = m * seq + t
+            at = pl.multiple_of(row * 16, 16)
+            b_in, c_out = b_ref[pl.ds(at, 16), :], c_ref[pl.ds(at, 16), :]
+            b_in = jnp.concatenate([b_in] * (chans // 128), axis=1)
+            c_out = jnp.concatenate([c_out] * (chans // 128), axis=1)
+            state = (
+                jnp.exp(step_ref[pl.ds(row, 1), :] * negative) * states[m]
+                + du_ref[pl.ds(row, 1), :] * b_in
+            )
+            mixed_ref[pl.ds(row, 1), :] = jnp.sum(state * c_out, axis=0, keepdims=True)
+            after.append(state)
+        return tuple(after)
+
+    lax.fori_loop(
+        0, seq, advance, tuple(jnp.zeros((16, chans), f32) for _ in range(batches)), unroll=4
+    )
+    mixed = mixed_ref[...] + skip[...] * u
+    own[...] = (h + mixed * (u / (1.0 + jnp.exp(-u)))).astype(bf16)
+    relay_copy = remote(own, relay, relay_send, relay_recv, partner)
+    relay_copy.start()
+
+    def slot_arrived(n):
+        source = lax.rem(me + n, peers)
+        remote(
+            slot_buf.at[source], slot_buf.at[source], slot_send.at[0], slot_recv.at[source], (sec, me)
+        ).wait_recv()
+
+    loop(1, peers, slot_arrived)
+    slot_table = jnp.concatenate([slot_buf[n, :1, :] for n in range(peers)], axis=0).astype(bf16)
+    token = iota((1, 128), 1)
+    position, batch = token & (seq - 1), token // seq
+    j_row, token_at = iota((128, 128), 0), iota((128, 128), 1)
+    flat_first = ((token_at & 3) * 2 + token_at // seq) * 2
+    block_mask = iota((peers, 128), 0) == (iota((peers, 128), 1) & (seq - 1)) >> 2
+    slots = []
+    for k in range(2):
+        pick = jnp.where(j_row == flat_first + k, 1.0, 0.0).astype(bf16)
+        picked = jnp.dot(slot_table, pick, preferred_element_type=f32)
+        slots.append(jnp.sum(jnp.where(block_mask, picked, 0.0), axis=0, keepdims=True))
+
+    def placed(count, expert):
+        q, r = iota((count, 128), 0), iota((count, 128), 1)
+        wanted = ((expert + (q >> 5)) * 2 + (q & 1)).astype(f32)
+        same = ((q >> 1) & (peers - 1)) == (r & (seq - 1)) >> 2
+        return same & ((slots[0] == wanted) | (slots[1] == wanted))
+
+    place_all = jnp.where(placed(16 * peers, 0), 1.0, 0.0).astype(bf16)
+    q, r = iota((rows, rows), 0), iota((rows, rows), 1)
+    regroup = jnp.where(
+        r == ((q >> 2) & 1) * seq + (q >> 3) * 4 + (q & 3), 1.0, 0.0
+    ).astype(bf16)
+
+    @pl.when(sec == 0)
+    def _():
+        relay_copy.wait_recv()
+
+    final = jnp.where(sec == 0, relay[...].astype(f32), own[...].astype(f32))
+    own_at = pl.multiple_of(me * chans, chans)
+    final_scaled = (final * moe_gain[:, pl.ds(own_at, chans)]).astype(bf16)
+    squares = jnp.sum(final * final, axis=1, keepdims=True)
+    third[...] = jnp.where(lanes == 8, squares, 0.0)
+    third[:, :8] = jnp.dot(
+        final_scaled, router[pl.ds(own_at, chans), :], preferred_element_type=f32
+    )
+    stat_buf[me] = jnp.transpose(third[...])[:16]
+
+    def stat_copy(n):
+        return remote(
+            stat_buf.at[me], stat_buf.at[me], stat_send.at[n], stat_recv.at[me],
+            (sec, lax.rem(me + n, peers)),
+        )
+
+    xsend[...] = jnp.dot(place_all, final_scaled, preferred_element_type=f32).astype(bf16)
+    rsend[...] = jnp.dot(regroup, final.astype(bf16), preferred_element_type=f32)
+    to_section = me // chips
+    column = pl.multiple_of(lax.rem(me, chips) * chans, chans)
+
+    def x_copy(n):
+        chip = lax.rem(me // 2 + n, chips)
+        at = pl.multiple_of(chip * 32, 32)
+        return remote(
+            xsend.at[pl.ds(at, 32)], xrow.at[:, pl.ds(column, chans)], x_send.at[n],
+            x_recv.at[lax.rem(me, chips)], (to_section, chip * 2 + sec),
+        )
+
+    def r_copy(n):
+        block = lax.rem(me // 2 + n, chips) * 2 + sec
+        at = pl.multiple_of(block * 8, 8)
+        return remote(
+            rsend.at[pl.ds(at, 8)], resid.at[:, pl.ds(column, chans)], r_send.at[n],
+            r_recv.at[lax.rem(me, chips)], (to_section, block),
+        )
+
+    itself = (to_section == sec) & (lax.rem(me, 2) == sec)
+
+    @pl.when(itself)
+    def _():
+        xrow[:, pl.ds(column, chans)] = xsend[pl.ds(pl.multiple_of(me // 2 * 32, 32), 32), :]
+        resid[:, pl.ds(column, chans)] = rsend[pl.ds(pl.multiple_of(me * 8, 8), 8), :]
+
+    @pl.when(jnp.logical_not(itself))
+    def _():
+        x_copy(0).start()
+
+    loop(1, chips, lambda n: x_copy(n).start())
+    loop(1, peers, lambda n: stat_copy(n).start())
+
+    @pl.when(jnp.logical_not(itself))
+    def _():
+        r_copy(0).start()
+
+    loop(1, chips, lambda n: r_copy(n).start())
+
+    def x_arrived(j):
+        @pl.when(jnp.logical_not(itself & (j == lax.rem(me, chips))))
+        def _():
+            at = pl.multiple_of(j * chans, chans)
+            remote(
+                xsend.at[pl.ds(0, 32)], xrow.at[:, pl.ds(at, chans)], x_send.at[0], x_recv.at[j],
+                (sec, me),
+            ).wait_recv()
+
+    def r_arrived(j):
+        @pl.when(jnp.logical_not(itself & (j == lax.rem(me, chips))))
+        def _():
+            at = pl.multiple_of(j * chans, chans)
+            remote(
+                rsend.at[pl.ds(0, 8)], resid.at[:, pl.ds(at, chans)], r_send.at[0], r_recv.at[j],
+                (sec, me),
+            ).wait_recv()
+
+    def stat_arrived(n):
+        source = lax.rem(me + n, peers)
+        remote(
+            stat_buf.at[source], stat_buf.at[source], stat_send.at[0], stat_recv.at[source], (sec, me)
+        ).wait_recv()
+
+    loop(1, peers, stat_arrived)
+    stats = jnp.sum(stat_buf[...], axis=0)
+    token_scale = lax.rsqrt(stats[8:9] / full + 1e-05)
+    logits = stats[:8] * token_scale
+    exps = jnp.exp(logits - jnp.max(logits, axis=0, keepdims=True))
+    probs = exps / jnp.sum(exps, axis=0, keepdims=True)
+    expert_row = iota((8, 128), 0)
+    chosen = [
+        jnp.sum(
+            jnp.where(expert_row == slots[k].astype(jnp.int32) >> 1, probs, 0.0),
+            axis=0, keepdims=True,
+        )
+        for k in range(2)
+    ]
+    both = chosen[0] + chosen[1]
+    weights = [chosen[k] / both for k in range(2)]
+    row_scale = jnp.sum(
+        jnp.where(placed(32, me // 2), token_scale, 0.0), axis=1, keepdims=True
+    )
+    loop(0, chips, x_arrived)
+
+    def part_copy(n):
+        return remote(parts.at[n], theirs.at[n], p_send.at[n], p_recv.at[n], partner)
+
+    def first_matmuls(n):
+        slot = lax.rem(n, IN_SLOTS)
+        in_copy(n).wait()
+        for g in range(2):
+            product = jnp.dot(xrow[...], win[slot, g], preferred_element_type=f32)
+            parts[n, g] = (product * row_scale).astype(bf16)
+
+        @pl.when(n < half)
+        def _():
+            part_copy(n).start()
+
+        @pl.when(n + IN_SLOTS < steps)
+        def _():
+            in_copy(n + IN_SLOTS).start()
+
+    loop(0, steps, first_matmuls)
+
+    def unit_copy(k):
+        return remote(units.at[k], units.at[half + k], u_send.at[k], u_recv.at[k], partner)
+
+    def down_matmul(n):
+        slot = lax.rem(n, OUT_SLOTS)
+        out_copy(n).wait()
+        acc[...] += jnp.dot(units[n], wout[slot], preferred_element_type=f32)
+
+        @pl.when(n + OUT_SLOTS < steps)
+        def _():
+            out_copy(n + OUT_SLOTS).start()
+
+    acc[...] = jnp.zeros_like(acc)
+
+    def own_units(k):
+        part_copy(k).wait_recv()
+        gate = parts[half + k, 0].astype(f32) + theirs[k, 0].astype(f32)
+        up = parts[half + k, 1].astype(f32) + theirs[k, 1].astype(f32)
+        units[k] = (gate / (1.0 + jnp.exp(-gate)) * up).astype(bf16)
+        unit_copy(k).start()
+        down_matmul(k)
+
+    loop(0, half, own_units)
+
+    def other_units(k):
+        unit_copy(k).wait_recv()
+        down_matmul(half + k)
+
+    loop(0, half, other_units)
+
+    pieces = acc.shape[1] // chans
+    stacked = jnp.concatenate(
+        [acc[:, f * chans:(f + 1) * chans] for f in range(pieces)], axis=0
+    ).astype(bf16)
+    count = 32 * pieces
+    q, z = iota((count, count), 0), iota((count, count), 1)
+    order = jnp.where(
+        z == (q & 7) * 32 + (q >> 4) * 2 + ((q >> 3) & 1), 1.0, 0.0
+    ).astype(bf16)
+    ret[...] = jnp.dot(order, stacked, preferred_element_type=f32).astype(bf16)
+
+    def back_copy(n):
+        block = lax.rem(me + n, peers)
+        to = pl.multiple_of(block * 16, 16)
+        at = pl.multiple_of(me * 16, 16)
+        return remote(
+            ret.at[pl.ds(to, 16)], back.at[pl.ds(at, 16)], b_send.at[n], b_recv.at[me], (sec, block)
+        )
+
+    loop(1, peers, lambda n: back_copy(n).start())
+    mine_at = pl.multiple_of(me * 16, 16)
+    back[pl.ds(mine_at, 16), :] = ret[pl.ds(mine_at, 16), :]
+
+    tok, lane64 = iota((64, 128), 0) & 7, iota((64, 128), 1)
+    here = lane64 == (tok >> 2) * seq + me * 4 + (tok & 3)
+    mix_row, mix_lane = iota((64, 256), 0), iota((64, 256), 1)
+    slot_of = ((mix_lane >> 5) * 2 + ((mix_lane >> 3) & 1)).astype(f32)
+    aligned = (mix_row >> 3) == (mix_lane & 7)
+    mix = jnp.zeros((64, 256), f32)
+    for k in range(2):
+        weight = jnp.sum(jnp.where(here, weights[k], 0.0), axis=1, keepdims=True)
+        slot = jnp.sum(jnp.where(here, slots[k], 0.0), axis=1, keepdims=True)
+        mix = mix + jnp.where(aligned & (slot == slot_of), weight, 0.0)
+    mix_high = mix.astype(bf16)
+    mix_low = (mix - mix_high.astype(f32)).astype(bf16)
+    loop(0, chips, r_arrived)
+
+    def back_arrived(n):
+        source = lax.rem(me + n, peers)
+        at = pl.multiple_of(source * 16, 16)
+        remote(
+            ret.at[pl.ds(0, 16)], back.at[pl.ds(at, 16)], b_send.at[0], b_recv.at[source], (sec, me)
+        ).wait_recv()
+
+    loop(1, peers, back_arrived)
+    routed = jnp.dot(mix_high, back[...], preferred_element_type=f32) + jnp.dot(
+        mix_low, back[...], preferred_element_type=f32
+    )
+    for f in range(pieces):
+        columns = slice(f * chans, (f + 1) * chans)
+        value = (resid[:, columns] + routed[f * 8:(f + 1) * 8]).astype(bf16)
+        out[0, :, columns] = value[:4]
+        out[1, :, columns] = value[4:]
+
+    @pl.when(odd)
+    def _():
+        rs_copy(0).wait_send()
+
+    loop(1, chips, lambda n: rs_copy(n).wait_send())
+
+    @pl.when(jnp.logical_not(odd))
+    def _():
+        loop(1, peers, lambda n: ag_copy(n).wait_send())
+
+    @pl.when(jnp.logical_not(itself))
+    def _():
+        x_copy(0).wait_send()
+        r_copy(0).wait_send()
+
+    def x_left(n):
+        x_copy(n).wait_send()
+        r_copy(n).wait_send()
+
+    loop(1, chips, x_left)
+
+    def rest_left(n):
+        slot_copy(n).wait_send()
+        stat_copy(n).wait_send()
+        back_copy(n).wait_send()
+
+    loop(1, peers, rest_left)
+
+    def halves_left(k):
+        part_copy(k).wait_send()
+        unit_copy(k).wait_send()
+
+    loop(0, half, halves_left)
+    relay_copy.wait_send()
+
+
+def scaled_of(h, scale, gain):
+    return h * scale * gain
+
+
+def fused(
+    inputs, expert_ids, mamba_gain, dt_in, dt_out, dt_bias, state_in, decay_rate, skip_gain,
+    moe_gain, router, expert_in, expert_out,
+):
+    f32, bf16 = jnp.float32, jnp.bfloat16
+    peers = lax.axis_size("expert")
+    batches, seq, chans = inputs.shape
+    rows = batches * seq
+    depth, columns = expert_in.shape[1:]
+    steps = columns // STEP_COLUMNS
+    half = steps // 2
+    chips = peers // 2
+    vmem = pl.BlockSpec(memory_space=pltpu.VMEM)
+    smem = pl.BlockSpec(memory_space=pltpu.SMEM)
+    hbm = pl.BlockSpec(memory_space=pl.ANY)
+    dma = pltpu.SemaphoreType.DMA
+    scratch = [
+        pltpu.VMEM((IN_SLOTS, 2, depth, STEP_COLUMNS), bf16),
+        pltpu.VMEM((OUT_SLOTS, STEP_COLUMNS, depth), bf16),
+        pltpu.VMEM((rows, WIDE), bf16),
+        pltpu.VMEM((peers, 16, WIDE), bf16),
+        pltpu.VMEM((16, WIDE), bf16),
+        pltpu.VMEM((rows, WIDE), bf16),
+        pltpu.VMEM((rows, 128), f32),
+        pltpu.VMEM((rows, chans), f32),
+        pltpu.VMEM((rows, chans), f32),
+        pltpu.VMEM((rows, chans), f32),
+        pltpu.VMEM((rows * 16, 128), f32),
+        pltpu.VMEM((rows * 16, 128), f32),
+        pltpu.VMEM((rows, chans), bf16),
+        pltpu.VMEM((rows, chans), bf16),
+        pltpu.VMEM((peers, 8, 128), f32),
+        pltpu.VMEM((peers, 16, 128), f32),
+        pltpu.VMEM((16 * peers, chans), bf16),
+        pltpu.VMEM((32, depth), bf16),
+        pltpu.VMEM((rows, chans), f32),
+        pltpu.VMEM((8, depth), f32),
+        pltpu.VMEM((steps, 2, 32, STEP_COLUMNS), bf16),
+        pltpu.VMEM((half, 2, 32, STEP_COLUMNS), bf16),
+        pltpu.VMEM((steps, 32, STEP_COLUMNS), bf16),
+        pltpu.VMEM((32, depth), f32),
+        pltpu.VMEM((16 * peers, chans), bf16),
+        pltpu.VMEM((16 * peers, chans), bf16),
+        dma((IN_SLOTS,)), dma((OUT_SLOTS,)),
+        dma((chips,)), dma((peers,)), dma((peers,)), dma((chips,)), dma, dma,
+        dma((peers,)), dma((peers,)), dma((peers,)), dma((peers,)),
+        dma((chips,)), dma((chips,)), dma((chips,)), dma((chips,)),
+        dma((half,)), dma((half,)), dma((half,)), dma((half,)),
+        dma((peers,)), dma((peers,)),
+    ]
+    return pl.pallas_call(
+        kernel,
+        out_shape=jax.ShapeDtypeStruct((batches, seq // peers, depth), bf16),
+        in_specs=[vmem, smem] + [vmem] * 9 + [hbm, hbm],
+        out_specs=vmem,
+        scratch_shapes=scratch,
+        compiler_params=pltpu.CompilerParams(
+            collective_id=0, has_side_effects=True, vmem_limit_bytes=62 << 20
+        ),
+    )(
+        inputs, expert_ids, mamba_gain, dt_in, dt_out, dt_bias, state_in, decay_rate, skip_gain,
+        moe_gain.reshape(1, -1), router, expert_in, expert_out,
+    )
+
+
+def fits(mesh):
+    return mesh.shape["section"] == 2 and mesh.shape["expert"] == 16
+
+
 def solution(mesh):
     placed = (
         P(None, None, "expert"),
@@ -189,6 +751,7 @@
         P(None, "section", "expert"),
         P("expert", "section"),
     )
+    body = fused if fits(mesh) else shards
     return jax.shard_map(
-        shards, mesh=mesh, in_specs=placed, out_specs=P(None, "expert", "section"), check_vma=False
-    )
+        body, mesh=mesh, in_specs=placed, out_specs=P(None, "expert", "section"), check_vma=False
+    )

time: 508 us -> 79.3 us (0.16); the launches traced: 501 us -> 79 us
  blocking collectives: 269 us -> 0 us
  waiting for transfers between devices: 75.2 us -> 0 us
  Pallas kernels: 0 us -> 71.1 us
  other arithmetic: 61.6 us -> 0 us
  matrix products: 45 us -> 0 us
  starting transfers between devices: 26.7 us -> 0 us
  between operations: 13.6 us -> 0.01 us
    psum x6 -> x0, blocking collectives: 269 us -> none  [the longest x3 175 us: mamba_layer(): low_sum, state_sum = lax.psum((low_part, state_part), 'expert')]
    pallas_call x0 -> x1, Pallas kernels: none -> 71.1 us  [fused(): pl.pallas_call(kernel, out_shape=jax.ShapeDtypeStruct((batches, seq // pe...]
    reduce_sum x69 -> x0, other arithmetic: 53.9 us -> none  [the longest x60 50.5 us: advance(): emitted.append(jnp.sum(carried * c_block[index][None, :], axis=1))]
    psum x2 -> x0, waiting for transfers between devices: 48.6 us -> none  [the longest x1 30.1 us: moe_layer(): lax.psum(up_part.astype(jnp.bfloat16), 'section').astype(jnp.float32)]
    dot_general x14 -> x0, matrix products: 45 us -> none  [the longest x1 12.8 us: moe_layer(): jnp.dot(units, out_w, preferred_element_type=jnp.float32)]
    all_to_all x3 -> x0, waiting for transfers between devices: 21.8 us -> none  [the longest x1 7.48 us: moe_layer(): lax.all_to_all(produced.reshape(devices, capacity, slice_width), 'expert'...]
    all_to_all x3 -> x0, starting transfers between devices: 14.7 us -> none  [the longest x1 5.61 us: shards(): lax.all_to_all(finals, 'expert', split_axis=1, concat_axis=2, tiled=True)]
    ppermute x3 -> x0, starting transfers between devices: 11.9 us -> none  [passed_along(): return lax.ppermute(array, axis, pairs)]
  transfers between devices with their start and end apart: 8 -> 0, of which waited for: 8 -> 0; matrix products, arithmetic and copies ran while one was open for 1% -> 0% of each run, Pallas kernels for 0% -> 0%
where the time goes in v1:
time: 79.3 us; the launch traced here: 79 us
  Pallas kernels  71.1 us (90%)
  local copies, waits for them, and re-layouts  7.82 us (10%)
    pallas_call x1, Pallas kernels, fused(): pl.pallas_call(kernel, out_shape=jax.ShapeDtypeStruct((batches, seq // pe...  71.1 us
    unnamed x5, local copies, waits for them, and re-layouts  7.82 us

profile of v1, /device:TPU:0, one launch (start us, length us, event | category | flops | bytes accessed | tf_op | source)
XLA Modules:
  0.0 79.0 jit_solution(7782173358196076081)
XLA Ops:
  0.0 1.4 %copy.14.ids = s32[4,2,2]{2,1,0:T(2,128)} copy(s32[4,2,2]{0,2,1:T(2,128)} %param.14) | data formatting | bytes 128 | tf_op args[1]
  1.4 1.4 %copy.15.state_w = bf16[1,256,32]{2,1,0:T(8,128)(2,1)} copy(bf16[1,256,32]{1,2,0:T(8,128)(2,1)} %param.19) | data formatting | bytes 32768 | tf_op args[6]
  2.8 1.5 %copy.16.rate = f32[1,256,16]{2,1,0:T(8,128)} copy(f32[1,256,16]{1,2,0:T(8,128)} %param.20) | data formatting | bytes 32768 | tf_op args[7]
  4.3 2.2 %copy.17.router = bf16[4096,8]{1,0:T(8,128)(2,1)} copy(bf16[4096,8]{0,1:T(8,128)(2,1)} %param.23) | data formatting | bytes 131072 | tf_op args[10]
  6.4 71.1 %shard_map.127 = bf16[2,4,2048]{2,1,0:T(4,128)(2,1)} custom-call(bf16[2,64,256]{2,1,0:T(8,128)(2,1)} %inputs.1, s32[4,2,2]{2,1,0:T(2,128)} %copy.14.ids, f32[1,256]{1,0:T(1,128)} %gain.1, bf16[1,256,256]{2,1,0:T(8,128)(2,1)} %dt_in.1, bf16[1,256,256]{2,1,0:T(8,128)(2,1)} %dt_out.1, f32[1,256]{1,0:T(1,128)} %bias.1, bf16[1,256,32]{2,1,0:T(8,128)(2,1)} %copy.15.state_w, ...), custom_call_target="tpu_custom_call" | custom-call | tf_op jit(solution)/shard_map/pallas_call | solution.py:719
  77.6 1.4 %copy.19 = bf16[2,4,2048]{2,1,0:T(4,128)(2,1)} copy(bf16[2,4,2048]{2,1,0:T(4,128)(2,1)} %shard_map.127) | data formatting | bytes 65536

commit v2 on v1

--- a/solution.py
+++ b/solution.py
@@ -191,7 +191,7 @@
 def kernel(
     inputs, ids, gain, dt_in, dt_out, bias, state_w, rate, skip, moe_gain, router, w_in, w_out,
     out,
-    win, wout, part, rs_buf, summed, ag_buf, third, step_ref, du_ref, mixed_ref, b_ref, c_ref,
+    win, wout, part, rs_buf, summed, ag_buf, third, h_ref, step_ref, du_ref, mixed_ref, b_ref, c_ref,
     own, relay, slot_buf, stat_buf, xsend, xrow, rsend, resid, parts, theirs, units, acc, ret, back,
     in_sem, out_sem, rs_send, rs_recv, ag_send, ag_recv, relay_send, relay_recv,
     slot_send, slot_recv, stat_send, stat_recv, x_send, x_recv, r_send, r_recv,
@@ -201,6 +201,7 @@
     peers = lax.axis_size("expert")
     sec, me = lax.axis_index("section"), lax.axis_index("expert")
     partner = (1 - sec, me)
+    across_last = (((1,), (1,)), ((), ()))
     batches, seq, chans = inputs.shape
     rows = batches * seq
     chips = peers // 2
@@ -252,70 +253,77 @@
     lane, sub = iota((16, 128), 1), iota((16, 128), 0)
     across, down = jnp.full((16, 128), -1, jnp.int32), jnp.full((16, 128), -2, jnp.int32)
     for j in range(16):
-        value = ids[j // 4, (j // 2) % 2, j % 2]
+        value = ids[(j // 2) % 2, j % 2, j // 4]
         across = jnp.where(lane == j, value, across)
         down = jnp.where(sub == j, value, down)
     earlier = jnp.where((across == down) & (sub < lane), 1.0, 0.0)
     rank = jnp.sum(earlier, axis=0, keepdims=True)
     slot_row = across[:1].astype(f32) * 2.0 + rank
     slot_buf[me] = jnp.broadcast_to(slot_row, (8, 128))
-    pl.semaphore_wait(barrier, total - 1)
 
     def slot_copy(n):
         return remote(
             slot_buf.at[me], slot_buf.at[me], slot_send.at[n], slot_recv.at[me],
-            (sec, lax.rem(me + n, peers)),
-        )
-
-    loop(1, peers, lambda n: slot_copy(n).start())
+            (sec, exclusive(me, peers - n, peers)),
+        )
+
+    lanes = iota((rows, 128), 1)
+
+    def project(values):
+        h_ref[...] = values
+        scaled = (values * gain[...]).astype(bf16)
+        squares = jnp.sum(values * values, axis=1, keepdims=True)
+        high = squares.astype(bf16).astype(f32)
+        third[...] = jnp.where(lanes == 32, high, jnp.where(lanes == 33, squares - high, 0.0))
+        third[:, :32] = lax.dot_general(scaled, state_w[0], across_last, preferred_element_type=f32)
+        low = jnp.dot(scaled, dt_in[0], preferred_element_type=f32)
+        part[:, :256] = low.astype(bf16)
+        part[:, 256:] = third[...].astype(bf16)
+
+    project(inputs[...].reshape(rows, chans).astype(f32))
+    pl.semaphore_wait(barrier, total - 1)
 
     @pl.when(sec == 1)
     def _():
         remote(own, relay, relay_send, relay_recv, partner).wait_recv()
-
-    first = inputs[...].reshape(rows, chans)
-    h = jnp.where(sec == 0, first.astype(f32), relay[...].astype(f32))
-    scaled = h * gain[...]
-    scaled_b = scaled.astype(bf16)
-    squares = jnp.sum(h * h, axis=1, keepdims=True)
-    high = squares.astype(bf16).astype(f32)
-    lanes = iota((rows, 128), 1)
-    third[...] = jnp.where(lanes == 32, high, jnp.where(lanes == 33, squares - high, 0.0))
-    third[:, :32] = jnp.dot(scaled_b, state_w[0], preferred_element_type=f32)
-    low = jnp.dot(scaled_b, dt_in[0], preferred_element_type=f32)
-    part[:, :256] = low.astype(bf16)
-    part[:, 256:] = third[...].astype(bf16)
+        project(relay[...].astype(f32))
+
+    h = h_ref[...]
+
+    reducer = lax.rem(me, 2) == 0
+    share = me // 2
+
+    def rs_to(n):
+        return exclusive(share, lax.rem(chips - n, chips), chips)
 
     def rs_copy(n):
-        chip = lax.rem(me // 2 + n, chips)
-        at = pl.multiple_of(chip * 16, 16)
+        at = pl.multiple_of(rs_to(n) * 16, 16)
         return remote(
-            part.at[pl.ds(at, 16)], rs_buf.at[me], rs_send.at[n], rs_recv.at[me], (sec, chip * 2)
-        )
-
-    odd = lax.rem(me, 2) == 1
-
-    @pl.when(odd)
+            part.at[pl.ds(at, 16)], rs_buf.at[me], rs_send.at[n], rs_recv.at[me],
+            (sec, 2 * rs_to(n)),
+        )
+
+    @pl.when(jnp.logical_not(reducer))
     def _():
         rs_copy(0).start()
 
     loop(1, chips, lambda n: rs_copy(n).start())
 
+    share_at = pl.multiple_of(share * 16, 16)
+
     def ag_copy(n):
-        at = pl.multiple_of(me // 2 * 16, 16)
         return remote(
-            summed, ag_buf.at[pl.ds(at, 16)], ag_send.at[n], ag_recv.at[me // 2],
-            (sec, lax.rem(me + n, peers)),
+            summed, ag_buf.at[pl.ds(share_at, 16)], ag_send.at[n], ag_recv.at[share],
+            (sec, exclusive(me, peers - n, peers)),
         )
 
     def rs_arrived(source):
         return remote(part.at[pl.ds(0, 16)], rs_buf.at[source], rs_send.at[0], rs_recv.at[source], (sec, me))
 
-    @pl.when(jnp.logical_not(odd))
-    def _():
-        at = pl.multiple_of(me // 2 * 16, 16)
-        rs_buf[me] = part[pl.ds(at, 16), :]
-        loop(1, peers, lambda n: rs_arrived(lax.rem(me + n, peers)).wait_recv())
+    @pl.when(reducer)
+    def _():
+        rs_buf[me] = part[pl.ds(share_at, 16), :]
+        loop(1, peers, lambda n: rs_arrived(exclusive(me, peers - n, peers)).wait_recv())
         whole = jnp.sum(rs_buf[...].astype(f32), axis=0)
         square = whole[:, 288:289] + whole[:, 289:290]
         scale = lax.rsqrt(square / full + 1e-05)
@@ -325,18 +333,20 @@
             lane3 == 288, scale_high, jnp.where(lane3 == 289, scale - scale_high, whole * scale)
         )
         summed[...] = result.astype(bf16)
-        ag_buf[pl.ds(at, 16), :] = summed[...]
+        ag_buf[pl.ds(share_at, 16), :] = summed[...]
         loop(1, peers, lambda n: ag_copy(n).start())
+
+    loop(1, peers, lambda n: slot_copy(n).start())
 
     def ag_arrived(chip):
         at = pl.multiple_of(chip * 16, 16)
         return remote(summed, ag_buf.at[pl.ds(at, 16)], ag_send.at[0], ag_recv.at[chip], (sec, me))
 
-    @pl.when(odd)
-    def _():
-        ag_arrived(me // 2).wait_recv()
-
-    loop(1, chips, lambda n: ag_arrived(lax.rem(me // 2 + n, chips)).wait_recv())
+    @pl.when(jnp.logical_not(reducer))
+    def _():
+        ag_arrived(share).wait_recv()
+
+    loop(1, chips, lambda n: ag_arrived(rs_to(n)).wait_recv())
 
     tail = ag_buf[:, 256:]
     tail_f = tail.astype(f32)
@@ -359,7 +369,7 @@
         jnp.where(state_lane == state_row + 16, repeated, 0.0).astype(bf16), ones,
         preferred_element_type=f32,
     )
-    negative = -jnp.transpose(rate[0])
+    negative = -rate[0]
 
     def advance(t, states):
         after = []
@@ -386,7 +396,7 @@
     relay_copy.start()
 
     def slot_arrived(n):
-        source = lax.rem(me + n, peers)
+        source = exclusive(me, peers - n, peers)
         remote(
             slot_buf.at[source], slot_buf.at[source], slot_send.at[0], slot_recv.at[source], (sec, me)
         ).wait_recv()
@@ -425,15 +435,15 @@
     final_scaled = (final * moe_gain[:, pl.ds(own_at, chans)]).astype(bf16)
     squares = jnp.sum(final * final, axis=1, keepdims=True)
     third[...] = jnp.where(lanes == 8, squares, 0.0)
-    third[:, :8] = jnp.dot(
-        final_scaled, router[pl.ds(own_at, chans), :], preferred_element_type=f32
+    third[:, :8] = lax.dot_general(
+        final_scaled, router[:, pl.ds(own_at, chans)], across_last, preferred_element_type=f32
     )
     stat_buf[me] = jnp.transpose(third[...])[:16]
 
     def stat_copy(n):
         return remote(
             stat_buf.at[me], stat_buf.at[me], stat_send.at[n], stat_recv.at[me],
-            (sec, lax.rem(me + n, peers)),
+            (sec, exclusive(me, peers - n, peers)),
         )
 
     xsend[...] = jnp.dot(place_all, final_scaled, preferred_element_type=f32).astype(bf16)
@@ -442,7 +452,7 @@
     column = pl.multiple_of(lax.rem(me, chips) * chans, chans)
 
     def x_copy(n):
-        chip = lax.rem(me // 2 + n, chips)
+        chip = exclusive(me // 2, lax.rem(chips - n, chips), chips)
         at = pl.multiple_of(chip * 32, 32)
         return remote(
             xsend.at[pl.ds(at, 32)], xrow.at[:, pl.ds(column, chans)], x_send.at[n],
@@ -450,7 +460,7 @@
         )
 
     def r_copy(n):
-        block = lax.rem(me // 2 + n, chips) * 2 + sec
+        block = exclusive(me // 2, lax.rem(chips - n, chips), chips) * 2 + sec
         at = pl.multiple_of(block * 8, 8)
         return remote(
             rsend.at[pl.ds(at, 8)], resid.at[:, pl.ds(column, chans)], r_send.at[n],
@@ -496,7 +506,7 @@
             ).wait_recv()
 
     def stat_arrived(n):
-        source = lax.rem(me + n, peers)
+        source = exclusive(me, peers - n, peers)
         remote(
             stat_buf.at[source], stat_buf.at[source], stat_send.at[0], stat_recv.at[source], (sec, me)
         ).wait_recv()
@@ -584,7 +594,7 @@
     ret[...] = jnp.dot(order, stacked, preferred_element_type=f32).astype(bf16)
 
     def back_copy(n):
-        block = lax.rem(me + n, peers)
+        block = exclusive(me, peers - n, peers)
         to = pl.multiple_of(block * 16, 16)
         at = pl.multiple_of(me * 16, 16)
         return remote(
@@ -610,7 +620,7 @@
     loop(0, chips, r_arrived)
 
     def back_arrived(n):
-        source = lax.rem(me + n, peers)
+        source = exclusive(me, peers - n, peers)
         at = pl.multiple_of(source * 16, 16)
         remote(
             ret.at[pl.ds(0, 16)], back.at[pl.ds(at, 16)], b_send.at[0], b_recv.at[source], (sec, me)
@@ -626,13 +636,13 @@
         out[0, :, columns] = value[:4]
         out[1, :, columns] = value[4:]
 
-    @pl.when(odd)
+    @pl.when(jnp.logical_not(reducer))
     def _():
         rs_copy(0).wait_send()
 
     loop(1, chips, lambda n: rs_copy(n).wait_send())
 
-    @pl.when(jnp.logical_not(odd))
+    @pl.when(reducer)
     def _():
         loop(1, peers, lambda n: ag_copy(n).wait_send())
 
@@ -660,6 +670,14 @@
 
     loop(0, half, halves_left)
     relay_copy.wait_send()
+
+
+def exclusive(a, b, count):
+    total, bit = 0, 1
+    while bit < count:
+        total = total + lax.rem(a // bit + b // bit, 2) * bit
+        bit *= 2
+    return total
 
 
 def scaled_of(h, scale, gain):
@@ -690,6 +708,7 @@
         pltpu.VMEM((16, WIDE), bf16),
         pltpu.VMEM((rows, WIDE), bf16),
         pltpu.VMEM((rows, 128), f32),
+        pltpu.VMEM((rows, chans), f32),
         pltpu.VMEM((rows, chans), f32),
         pltpu.VMEM((rows, chans), f32),
         pltpu.VMEM((rows, chans), f32),
@@ -726,8 +745,9 @@
             collective_id=0, has_side_effects=True, vmem_limit_bytes=62 << 20
         ),
     )(
-        inputs, expert_ids, mamba_gain, dt_in, dt_out, dt_bias, state_in, decay_rate, skip_gain,
-        moe_gain.reshape(1, -1), router, expert_in, expert_out,
+        inputs, expert_ids.transpose(1, 2, 0), mamba_gain, dt_in, dt_out, dt_bias,
+        state_in.transpose(0, 2, 1), decay_rate.transpose(0, 2, 1), skip_gain,
+        moe_gain.reshape(1, -1), router.T, expert_in, expert_out,
     )
 
 

time: 79.3 us -> 71.1 us (0.90)
  local copies, waits for them, and re-layouts: 7.82 us -> 1.39 us
  Pallas kernels: 71.1 us -> 69.5 us
    unnamed x5 -> x1, local copies, waits for them, and re-layouts: 7.82 us -> 1.39 us
    pallas_call x1, Pallas kernels: 71.1 us -> 69.5 us  [fused(): pl.pallas_call(kernel, out_shape=jax.ShapeDtypeStruct((batches, seq // pe...]
where the time goes in v2:
time: 71.1 us; the launch traced here: 70.9 us
  Pallas kernels  69.5 us (98%)
  local copies, waits for them, and re-layouts  1.39 us (2%)
    pallas_call x1, Pallas kernels, fused(): pl.pallas_call(kernel, out_shape=jax.ShapeDtypeStruct((batches, seq // pe...  69.5 us

profile of v2, /device:TPU:0, one launch (start us, length us, event | category | flops | bytes accessed | tf_op | source)
XLA Modules:
  0.0 70.9 jit_solution(9662085191772998857)
XLA Ops:
  0.0 69.5 %shard_map.127 = bf16[2,4,2048]{2,1,0:T(4,128)(2,1)} custom-call(bf16[2,64,256]{2,1,0:T(8,128)(2,1)} %inputs.1, s32[2,2,4]{2,1,0:T(2,128)} %bitcast.9, f32[1,256]{1,0:T(1,128)} %gain.1, bf16[1,256,256]{2,1,0:T(8,128)(2,1)} %dt_in.1, bf16[1,256,256]{2,1,0:T(8,128)(2,1)} %dt_out.1, f32[1,256]{1,0:T(1,128)} %bias.1, bf16[1,32,256]{2,1,0:T(8,128)(2,1)} %bitcast.6, ...), custom_call_target="tpu_custom_call" | custom-call | tf_op jit(solution)/shard_map/pallas_call | solution.py:738
  69.5 1.4 %copy.15 = bf16[2,4,2048]{2,1,0:T(4,128)(2,1)} copy(bf16[2,4,2048]{2,1,0:T(4,128)(2,1)} %shard_map.127) | data formatting | bytes 65536
